TPU v7x, 512 devices: a whole 4x8x8 slice. The times are simulated.
512 devices in a mesh: expert: 2 (over y_hi), cfg: 2 (over core), rep: 16 (over x, y_lo), sp: 8 (over z).
Axes of the slice: x: 4, y: 8 (y_hi: 2, y_lo: 4; y = y_hi * 4 + y_lo), z: 8, core: 2. Of those that a mesh axis runs over, the one named last changes fastest.
Arguments:
- queries: bfloat16 [2, 2, 10240, 3072], P('expert', None, ('rep', 'cfg', 'sp')), parts along dimension 2, may hold values from -600 to 600
- keys: bfloat16 [2, 2, 10240, 3072], P('expert', None, ('rep', 'cfg', 'sp')), parts along dimension 2, may hold values from -600 to 600
- values: bfloat16 [2, 2, 10240, 3072], P('expert', None, ('rep', 'cfg', 'sp')), parts along dimension 2, may hold values from -600 to 600
- cross_queries: bfloat16 [2, 2, 10240, 3072], P('expert', None, ('rep', 'cfg', 'sp')), parts along dimension 2, may hold values from -600 to 600
- q_gain: float32 [2, 3072], P('expert'), may hold values from 0.1 to 1.9
- k_gain: float32 [2, 3072], P('expert'), may hold values from 0.1 to 1.9
- cross_gain: float32 [2, 3072], P('expert'), may hold values from 0.1 to 1.9
- text_keys: bfloat16 [2, 2, 4096, 3072], P('expert', 'cfg', 'rep', 'sp'), parts along dimension 2, may hold values from -48 to 48
- text_values: bfloat16 [2, 2, 4096, 3072], P('expert', 'cfg', 'rep', 'sp'), parts along dimension 2, may hold values from -5 to 5
- text_lengths: int32 [2, 2, 16], P('expert', 'cfg', 'rep'), parts along dimension 2, may hold values from 1 to 256, as said below
- step_index: int32 [2, 16], P('expert', 'rep'), parts along dimension 1, may hold values from 0 to 39, as said below
- latent: float32 [2, 10240, 64], P('expert', ('rep', 'cfg', 'sp')), parts along dimension 1, may hold values from -5 to 5
- head_weight: bfloat16 [2, 3072, 64], P('expert', 'sp'), may hold values from -0.109375 to 0.109375
Outputs:
- clean_estimate: float32 [2, 10240, 64], P('expert', ('rep', 'cfg', 'sp')), parts along dimension 1
- handed_latent: bfloat16 [2, 10240, 64], P('expert', ('rep', 'cfg', 'sp')), parts along dimension 1
- handed_keys: bfloat16 [2, 2, 4096, 3072], P('expert', 'cfg', 'rep', 'sp'), parts along dimension 2
- handed_values: bfloat16 [2, 2, 4096, 3072], P('expert', 'cfg', 'rep', 'sp'), parts along dimension 2
There are 16 independent parts, one for each index of `rep`. A program takes and returns all parts, laid end to end along the dimension named above; an argument that names none is the same for every part. Nothing has to cross between parts.
Inputs may be any that keep to these rules, and one draw needn't show every extreme that they name: `text_lengths`: one entry equals 256. `step_index`: entry 0, the high-noise batch, is below 26; entry 1 is 26 or more.
All inputs are finite; a program needn't handle non-finite values.
Results may differ from a plain program's by a relative error of at most 0.0068.
Values may be sent and summed in bfloat16 or wider, within the bound.
A program may use at most 64 MiB of HBM per device.

v0:
```python
import math

import jax
import jax.numpy as jnp
from jax import lax
from jax.sharding import PartitionSpec as P

HEAD = 128
STEPS = 40


TIME_SHIFT = 12.0
HIGH_GUIDE = 4.0
LOW_GUIDE = 3.0
NORM_EPS = 1e-06


def swapped(value, axis, apart):
    mask = 2**apart
    pairs = [(source, source ^ mask) for source in range(lax.axis_size(axis))]
    return lax.ppermute(value, axis, pairs)


def sigma_at(index):
    frac = 1.0 - index.astype(jnp.float32) / STEPS
    return TIME_SHIFT * frac / (1.0 + (TIME_SHIFT - 1.0) * frac)


def rms_norm(features, gain_row):
    return (
        features
        * lax.rsqrt(jnp.mean(features * features, axis=-1, keepdims=True) + NORM_EPS)
        * gain_row
    )


def rotary(features, positions):
    column = jnp.arange(features.shape[-1])
    pair_index = (column % HEAD // 2).astype(jnp.float32)
    freq = jnp.exp(-(2.0 * pair_index / HEAD) * math.log(10000.0))
    angle = positions[:, None] * freq[None, :]
    partner = jnp.where(
        column % 2 == 0, -jnp.roll(features, -1, axis=-1), jnp.roll(features, 1, axis=-1)
    )
    return features * jnp.cos(angle) + partner * jnp.sin(angle)


def attend_block(query_heads, key_heads, value_heads, key_mask):
    scores = jnp.einsum(
        "qhd,khd->hqk", query_heads, key_heads, preferred_element_type=jnp.float32
    ) / math.sqrt(HEAD)
    scores = jnp.where(key_mask[None, None, :], scores, -jnp.inf)
    row_max = jnp.max(scores, axis=-1, keepdims=True)
    exponent = jnp.exp(scores - row_max)
    weights = (exponent / jnp.sum(exponent, axis=-1, keepdims=True)).astype(jnp.bfloat16)
    return jnp.einsum("hqk,khd->qhd", weights, value_heads, preferred_element_type=jnp.float32)


def attention(query_heads, key_heads, value_heads, key_mask):
    return attend_block(query_heads, key_heads, value_heads, key_mask)


def per_device(
    queries,
    keys,
    values,
    cross_queries,
    q_gain,
    k_gain,
    cross_gain,
    text_keys,
    text_values,
    text_lengths,
    step_index,
    latent,
    head_weight,
):
    sp_count = lax.axis_size("sp")
    tok_rows = queries.shape[2]
    width = queries.shape[3]
    local_width = text_keys.shape[3]
    local_heads = local_width // HEAD
    text_count = text_keys.shape[2]
    seq_rows = sp_count * 2 * tok_rows
    block_index = lax.axis_index("cfg") * sp_count + lax.axis_index("sp")
    positions = (block_index * tok_rows + jnp.arange(tok_rows)).astype(jnp.float32)
    query_rot = rotary(rms_norm(queries[0].astype(jnp.float32), q_gain[0]), positions).astype(
        jnp.bfloat16
    )
    key_rot = rotary(rms_norm(keys[0].astype(jnp.float32), k_gain[0]), positions).astype(
        jnp.bfloat16
    )
    cross_norm = rms_norm(cross_queries[0].astype(jnp.float32), cross_gain[0]).astype(jnp.bfloat16)

    def split_heads(features):
        return features.reshape(2, 1, 1, tok_rows, sp_count, local_width)

    moved = (
        lax.all_to_all(
            lax.all_to_all(split_heads(query_rot), "cfg", split_axis=0, concat_axis=2, tiled=True),
            "sp",
            split_axis=4,
            concat_axis=1,
            tiled=True,
        ),
        lax.all_to_all(
            lax.all_to_all(split_heads(key_rot), "cfg", split_axis=0, concat_axis=2, tiled=True),
            "sp",
            split_axis=4,
            concat_axis=1,
            tiled=True,
        ),
        lax.all_to_all(
            lax.all_to_all(split_heads(values[0]), "cfg", split_axis=0, concat_axis=2, tiled=True),
            "sp",
            split_axis=4,
            concat_axis=1,
            tiled=True,
        ),
        lax.all_to_all(
            lax.all_to_all(split_heads(cross_norm), "cfg", split_axis=0, concat_axis=2, tiled=True),
            "sp",
            split_axis=4,
            concat_axis=1,
            tiled=True,
        ),
    )
    head_shape = (seq_rows, local_heads, HEAD)
    query_heads = moved[0].reshape(head_shape)
    key_heads = moved[1].reshape(head_shape)
    value_heads = moved[2].reshape(head_shape)
    cross_heads = moved[3].reshape(head_shape)
    text_rows = jnp.arange(text_count)
    text_mask = text_rows < text_lengths[0, 0, 0]
    text_shape = (text_count, local_heads, HEAD)
    self_out = attention(query_heads, key_heads, value_heads, jnp.ones((seq_rows,), dtype=bool))
    cross_out = attention(
        cross_heads,
        text_keys[0, 0].reshape(text_shape),
        text_values[0, 0].reshape(text_shape),
        text_mask,
    )
    hidden = lax.optimization_barrier(
        (self_out + cross_out).reshape(seq_rows, local_width).astype(jnp.bfloat16)
    )
    returned = lax.all_to_all(
        lax.all_to_all(
            hidden.reshape(1, sp_count, 2, tok_rows, 1, local_width),
            "cfg",
            split_axis=2,
            concat_axis=0,
            tiled=True,
        ),
        "sp",
        split_axis=1,
        concat_axis=4,
        tiled=True,
    )
    full_hidden = returned.reshape(2 * tok_rows, width).astype(jnp.float32)
    centred = full_hidden - jnp.mean(full_hidden, axis=-1, keepdims=True)
    normed = centred * lax.rsqrt(jnp.mean(centred * centred, axis=-1, keepdims=True) + NORM_EPS)
    velocity = jnp.dot(
        normed,
        lax.all_gather(head_weight[0], "sp", axis=0, tiled=True).astype(jnp.float32),
        precision=lax.Precision.HIGHEST,
    ).reshape(2, tok_rows, -1)
    guide_scale = jnp.where(lax.axis_index("expert") == 0, HIGH_GUIDE, LOW_GUIDE)
    guided = velocity[1] + guide_scale * (velocity[0] - velocity[1])
    sigma_now = sigma_at(step_index[0, 0])
    sigma_next = sigma_at(step_index[0, 0] + 1)
    clean_estimate = latent[0] - sigma_now * guided
    stepped = (latent[0] + (sigma_next - sigma_now) * guided).astype(jnp.bfloat16)
    keep_rows = text_mask[:, None]
    kept_keys = jnp.where(keep_rows, text_keys[0, 0], jnp.zeros_like(text_keys[0, 0]))
    kept_values = jnp.where(keep_rows, text_values[0, 0], jnp.zeros_like(text_values[0, 0]))
    handed = swapped((stepped, kept_keys, kept_values), "expert", 0)
    return (clean_estimate[None], handed[0][None], handed[1][None, None], handed[2][None, None])


def solution(mesh):
    in_specs = (
        P("expert", None, ("rep", "cfg", "sp"), None),
        P("expert", None, ("rep", "cfg", "sp"), None),
        P("expert", None, ("rep", "cfg", "sp"), None),
        P("expert", None, ("rep", "cfg", "sp"), None),
        P("expert", None),
        P("expert", None),
        P("expert", None),
        P("expert", "cfg", "rep", "sp"),
        P("expert", "cfg", "rep", "sp"),
        P("expert", "cfg", "rep"),
        P("expert", "rep"),
        P("expert", ("rep", "cfg", "sp"), None),
        P("expert", "sp", None),
    )
    out_specs = (
        P("expert", ("rep", "cfg", "sp"), None),
        P("expert", ("rep", "cfg", "sp"), None),
        P("expert", "cfg", "rep", "sp"),
        P("expert", "cfg", "rep", "sp"),
    )
    return jax.shard_map(
        per_device, mesh=mesh, in_specs=in_specs, out_specs=out_specs, check_vma=False
    )
```

profile of v0, /device:TPU:6, one launch (start us, length us, event | category | flops | bytes accessed | tf_op | source)
XLA Modules:
  0.0 197.3 jit_solution(822354674540912617)
XLA Ops:
  4.0 1.6 fusion.70
  12.4 1.8 multiply_cosine_fusion
  15.6 3.5 %all-to-all-start = ((bf16[2,1,1,40,8,384]{5,3,4,2,1,0:T(8,128)(2,1)}), bf16[2,1,1,40,8,384]{5,3,4,2,1,0:T(8,128)(2,1)S(1)}, u32[]{:S(2)}, u32[]{:S(2)}) async-start(bf16[2,1,1,40,8,384]{5,3,4,2,1,0:T(8,128)(2,1)} %copy.68), calls=%async_computation | async-start | bytes 983040 | tf_op jit(solution)/shard_map/all_to_all | solution.py:100
  20.8 3.5 %all-to-all-start.2 = ((bf16[2,1,1,40,8,384]{5,3,4,2,1,0:T(8,128)(2,1)}), bf16[2,1,1,40,8,384]{5,3,4,2,1,0:T(8,128)(2,1)S(1)}, u32[]{:S(2)}, u32[]{:S(2)}) async-start(bf16[2,1,1,40,8,384]{5,3,4,2,1,0:T(8,128)(2,1)} %copy.70), calls=%async_computation.2 | async-start | bytes 983040 | tf_op jit(solution)/shard_map/all_to_all | solution.py:107
  26.5 4.1 %all_to_all.135 = bf16[2,1,1,40,8,384]{5,3,4,2,1,0:T(8,128)(2,1)S(1)} all-to-all(bf16[2,1,1,40,8,384]{5,3,4,2,1,0:T(8,128)(2,1)S(1)} %copy.74), channel_id=1, replica_groups=mesh['expert'=2,'cfg'=2,'rep'=16,'sp'=8] {'cfg'}, dimensions={0} | all-to-all | bytes 983040 | tf_op jit(solution)/shard_map/all_to_all | solution.py:114
  30.6 4.1 %all_to_all.136 = bf16[2,1,1,40,8,384]{5,3,4,2,1,0:T(8,128)(2,1)S(1)} all-to-all(bf16[2,1,1,40,8,384]{5,3,4,2,1,0:T(8,128)(2,1)S(1)} %copy.78), channel_id=1, replica_groups=mesh['expert'=2,'cfg'=2,'rep'=16,'sp'=8] {'cfg'}, dimensions={0} | all-to-all | bytes 983040 | tf_op jit(solution)/shard_map/all_to_all | solution.py:121
  34.7 10.3 %all-to-all-start.1 = ((bf16[1,1,2,40,8,384]{5,3,2,1,0,4:T(8,128)(2,1)}), bf16[1,1,2,40,8,384]{5,3,2,1,0,4:T(8,128)(2,1)S(1)}, u32[]{:S(2)}, u32[]{:S(2)}) async-start(bf16[1,1,2,40,8,384]{5,3,2,1,0,4:T(8,128)(2,1)} %copy.69), calls=%async_computation.1 | async-start | bytes 983040 | tf_op jit(solution)/shard_map/all_to_all | solution.py:99
  45.9 16.3 %all-to-all-done.1 = bf16[1,1,2,40,8,384]{5,3,2,1,0,4:T(8,128)(2,1)S(1)} async-done(((bf16[1,1,2,40,8,384]{5,3,2,1,0,4:T(8,128)(2,1)}), bf16[1,1,2,40,8,384]{5,3,2,1,0,4:T(8,128)(2,1)S(1)}, u32[]{:S(2)}, u32[]{:S(2)}) %all-to-all-start.1) | async-done | bytes 491552 | tf_op jit(solution)/shard_map/all_to_all | solution.py:99
  62.1 3.5 %all-to-all-start.3 = ((bf16[1,1,2,40,8,384]{5,3,2,1,0,4:T(8,128)(2,1)}), bf16[1,1,2,40,8,384]{5,3,2,1,0,4:T(8,128)(2,1)S(1)}, u32[]{:S(2)}, u32[]{:S(2)}) async-start(bf16[1,1,2,40,8,384]{5,3,2,1,0,4:T(8,128)(2,1)} %copy.71), calls=%async_computation.3 | async-start | bytes 983040 | tf_op jit(solution)/shard_map/all_to_all | solution.py:106
  66.5 16.3 %all-to-all-done.3 = bf16[1,1,2,40,8,384]{5,3,2,1,0,4:T(8,128)(2,1)S(1)} async-done(((bf16[1,1,2,40,8,384]{5,3,2,1,0,4:T(8,128)(2,1)}), bf16[1,1,2,40,8,384]{5,3,2,1,0,4:T(8,128)(2,1)S(1)}, u32[]{:S(2)}, u32[]{:S(2)}) %all-to-all-start.3) | async-done | bytes 491552 | tf_op jit(solution)/shard_map/all_to_all | solution.py:106
  82.8 3.5 %all-to-all-start.5 = ((bf16[1,1,2,40,8,384]{5,3,2,1,0,4:T(8,128)(2,1)}), bf16[1,1,2,40,8,384]{5,3,2,1,0,4:T(8,128)(2,1)S(1)}, u32[]{:S(2)}, u32[]{:S(2)}) async-start(bf16[1,1,2,40,8,384]{5,3,2,1,0,4:T(8,128)(2,1)} %copy.75), calls=%async_computation.5 | async-start | bytes 983040 | tf_op jit(solution)/shard_map/all_to_all | solution.py:113
  87.1 16.3 %all-to-all-done.5 = bf16[1,1,2,40,8,384]{5,3,2,1,0,4:T(8,128)(2,1)S(1)} async-done(((bf16[1,1,2,40,8,384]{5,3,2,1,0,4:T(8,128)(2,1)}), bf16[1,1,2,40,8,384]{5,3,2,1,0,4:T(8,128)(2,1)S(1)}, u32[]{:S(2)}, u32[]{:S(2)}) %all-to-all-start.5) | async-done | bytes 491552 | tf_op jit(solution)/shard_map/all_to_all | solution.py:113
  103.4 3.5 %all-to-all-start.7 = ((bf16[1,1,2,40,8,384]{5,3,2,1,0,4:T(8,128)(2,1)}), bf16[1,1,2,40,8,384]{5,3,2,1,0,4:T(8,128)(2,1)S(1)}, u32[]{:S(2)}, u32[]{:S(2)}) async-start(bf16[1,1,2,40,8,384]{5,3,2,1,0,4:T(8,128)(2,1)} %copy.79), calls=%async_computation.7 | async-start | bytes 983040 | tf_op jit(solution)/shard_map/all_to_all | solution.py:120
  109.2 14.9 %all-to-all-done.7 = bf16[1,1,2,40,8,384]{5,3,2,1,0,4:T(8,128)(2,1)S(1)} async-done(((bf16[1,1,2,40,8,384]{5,3,2,1,0,4:T(8,128)(2,1)}), bf16[1,1,2,40,8,384]{5,3,2,1,0,4:T(8,128)(2,1)S(1)}, u32[]{:S(2)}, u32[]{:S(2)}) %all-to-all-start.7) | async-done | bytes 491552 | tf_op jit(solution)/shard_map/all_to_all | solution.py:120
  125.1 5.0 %fusion.73 = (f32[3,640]{1,0:T(4,128)S(1)}, f32[3,640,640]{1,2,0:T(8,128)}) fusion(bf16[640,3,128]{2,1,0:T(4,128)(2,1)} %reshape.391, bf16[640,3,128]{2,1,0:T(4,128)(2,1)S(1)} %reshape.390), kind=kOutput, calls=%fused_computation.101 | convolution fusion | flops 318259840 | bytes 5905920 | tf_op jit(solution)/shard_map/sub | solution.py:54
  130.1 3.1 %fusion.6 = f32[3,640,128]{1,2,0:T(8,128)S(1)} fusion(f32[3,640,640]{1,2,0:T(8,128)} %get-tuple-element.37, f32[3,640]{1,0:T(4,128)S(1)} %get-tuple-element.36, bf16[640,3,128]{2,1,0:T(4,128)(2,1)S(1)} %reshape.392), kind=kOutput, calls=%fused_computation.7 | convolution fusion | flops 317030400 | bytes 6397440 | tf_op jit(solution)/shard_map/hqk,khd->qhd/dot_general | solution.py:56
  133.2 2.1 %fusion.82 = (f32[3,640]{1,0:T(4,128)S(1)}, f32[3,640,256]{1,2,0:T(8,128)}) fusion(pred[256]{0:T(512)(128)(4,1)S(1)} %iota_compare_fusion, bf16[256,3,128]{0,2,1:T(8,128)(2,1)S(1)} %bitcast.178, bf16[640,3,128]{2,1,0:T(4,128)(2,1)S(1)} %copy-done.9), kind=kOutput, calls=%fused_computation.102 | convolution fusion | flops 127795456 | bytes 2662144 | tf_op jit(solution)/shard_map/sub | solution.py:54
  135.3 1.9 fusion.8
  137.6 4.3 %all_to_all.137 = bf16[1,8,2,40,1,384]{5,3,1,4,0,2:T(8,128)(2,1)S(1)} all-to-all(bf16[1,8,2,40,1,384]{5,3,1,4,0,2:T(8,128)(2,1)S(1)} %copy.86), channel_id=1, replica_groups=mesh['expert'=2,'cfg'=2,'rep'=16,'sp'=8] {'cfg'}, dimensions={2} | all-to-all | bytes 983040 | tf_op jit(solution)/shard_map/all_to_all | solution.py:147
  142.7 3.5 %all-to-all-start.9 = ((bf16[2,8,1,40,1,384]{5,3,0,4,2,1:T(8,128)(2,1)}), bf16[2,8,1,40,1,384]{5,3,0,4,2,1:T(8,128)(2,1)S(1)}, u32[]{:S(2)}, u32[]{:S(2)}) async-start(bf16[2,8,1,40,1,384]{5,3,0,4,2,1:T(8,128)(2,1)} %copy.87), calls=%async_computation.9 | async-start | bytes 983040 | tf_op jit(solution)/shard_map/all_to_all | solution.py:146
  146.3 7.7 %collective-permute-start.1 = (bf16[256,384]{1,0:T(8,128)(2,1)S(1)}, bf16[256,384]{1,0:T(8,128)(2,1)S(1)}, u32[]{:S(2)}, u32[]{:S(2)}) collective-permute-start(bf16[256,384]{1,0:T(8,128)(2,1)S(1)} %get-tuple-element.35), channel_id=1, source_target_pairs={{0,256},{256,0},{1,257},{257,1},{2,258},{258,2},{3,259},{259,3},{4... | collective-permute-start | bytes 589832 | tf_op jit(solution)/shard_map/ppermute | solution.py:21
  154.0 2.0 %collective-permute-start.2 = (bf16[256,384]{1,0:T(8,128)(2,1)S(1)}, bf16[256,384]{1,0:T(8,128)(2,1)S(1)}, u32[]{:S(2)}, u32[]{:S(2)}) collective-permute-start(bf16[256,384]{1,0:T(8,128)(2,1)S(1)} %get-tuple-element.34), channel_id=1, source_target_pairs={{0,256},{256,0},{1,257},{257,1},{2,258},{258,2},{3,259},{259,3},{4... | collective-permute-start | bytes 589832 | tf_op jit(solution)/shard_map/ppermute | solution.py:21
  156.9 26.7 %all-gather = bf16[1,3072,64]{1,2,0:T(8,128)(2,1)S(1)} all-gather(bf16[1,384,64]{1,2,0:T(8,128)(2,1)S(1)} %copy-done.13), channel_id=2, replica_groups=mesh['expert'=2,'cfg'=2,'rep'=16,'sp'=8] {'sp'}, dimensions={1}, use_global_device_ids=true | all-gather | bytes 442368 | tf_op jit(solution)/shard_map/all_gather | solution.py:164
  185.7 7.8 %collective-permute-start = (bf16[40,64]{0,1:T(8,128)(2,1)S(1)}, bf16[40,64]{0,1:T(8,128)(2,1)S(1)}, u32[]{:S(2)}, u32[]{:S(2)}) collective-permute-start(bf16[40,64]{0,1:T(8,128)(2,1)S(1)} %get-tuple-element.30), channel_id=1, source_target_pairs={{0,256},{256,0},{1,257},{257,1},{2,258},{258,2},{3,259},{259,3},{4... | collective-permute-start | bytes 15368 | tf_op jit(solution)/shard_map/ppermute | solution.py:21
  (106 shorter events, 27.3 us)
Async XLA Ops:
  1.9 1.7 copy-start
  3.8 3.1 %copy-start.12 = (f32[1,3072]{1,0:T(1,128)S(1)}, f32[1,3072]{1,0:T(1,128)}, u32[]{:S(2)}) copy-start(f32[1,3072]{1,0:T(1,128)} %param.18) | copy-start | bytes 36868
  8.0 1.5 copy-start.5
  9.9 2.4 %copy-start.1 = (bf16[1,2,40,3072]{3,2,1,0:T(8,128)(2,1)S(1)}, bf16[1,2,40,3072]{3,2,1,0:T(8,128)(2,1)}, u32[]{:S(2)}) copy-start(bf16[1,2,40,3072]{3,2,1,0:T(8,128)(2,1)} %param.14) | copy-start | bytes 1474564
  12.2 2.0 %copy-start.2 = (f32[10,8,8,384]{3,2,1,0:T(8,128)S(1)}, f32[10,8,8,384]{3,2,1,0:T(8,128)}, u32[]{:S(2)}) copy-start(f32[10,8,8,384]{3,2,1,0:T(8,128)} %copy.96) | copy-start | bytes 2949124
  12.2 2.0 %copy-start.3 = (f32[10,8,8,384]{3,2,1,0:T(8,128)S(1)}, f32[10,8,8,384]{3,2,1,0:T(8,128)}, u32[]{:S(2)}) copy-start(f32[10,8,8,384]{3,2,1,0:T(8,128)} %copy.97) | copy-start | bytes 2949124
  14.7 10.4 %copy-start.10 = (bf16[1,2,40,3072]{3,2,1,0:T(8,128)(2,1)S(1)}, bf16[1,2,40,3072]{3,2,1,0:T(8,128)(2,1)}, u32[]{:S(2)}) copy-start(bf16[1,2,40,3072]{3,2,1,0:T(8,128)(2,1)} %param.15) | copy-start | bytes 1474564
  15.6 5.2 %all-to-all-start = ((bf16[2,1,1,40,8,384]{5,3,4,2,1,0:T(8,128)(2,1)}), bf16[2,1,1,40,8,384]{5,3,4,2,1,0:T(8,128)(2,1)S(1)}, u32[]{:S(2)}, u32[]{:S(2)}) async-start(bf16[2,1,1,40,8,384]{5,3,4,2,1,0:T(8,128)(2,1)} %copy.68), calls=%async_computation | async-start | bytes 983040 | tf_op jit(solution)/shard_map/all_to_all | solution.py:100
  19.1 6.2 %copy-start.15 = (f32[1,3072]{1,0:T(1,128)S(1)}, f32[1,3072]{1,0:T(1,128)}, u32[]{:S(2)}) copy-start(f32[1,3072]{1,0:T(1,128)} %param.19) | copy-start | bytes 36868
  19.1 6.9 %copy-start.6 = (bf16[1,2,40,3072]{3,2,1,0:T(8,128)(2,1)S(1)}, bf16[1,2,40,3072]{3,2,1,0:T(8,128)(2,1)}, u32[]{:S(2)}) copy-start(bf16[1,2,40,3072]{3,2,1,0:T(8,128)(2,1)} %param.16) | copy-start | bytes 1474564
  20.8 5.7 %all-to-all-start.2 = ((bf16[2,1,1,40,8,384]{5,3,4,2,1,0:T(8,128)(2,1)}), bf16[2,1,1,40,8,384]{5,3,4,2,1,0:T(8,128)(2,1)S(1)}, u32[]{:S(2)}, u32[]{:S(2)}) async-start(bf16[2,1,1,40,8,384]{5,3,4,2,1,0:T(8,128)(2,1)} %copy.70), calls=%async_computation.2 | async-start | bytes 983040 | tf_op jit(solution)/shard_map/all_to_all | solution.py:107
  34.7 27.4 %all-to-all-start.1 = ((bf16[1,1,2,40,8,384]{5,3,2,1,0,4:T(8,128)(2,1)}), bf16[1,1,2,40,8,384]{5,3,2,1,0,4:T(8,128)(2,1)S(1)}, u32[]{:S(2)}, u32[]{:S(2)}) async-start(bf16[1,1,2,40,8,384]{5,3,2,1,0,4:T(8,128)(2,1)} %copy.69), calls=%async_computation.1 | async-start | bytes 983040 | tf_op jit(solution)/shard_map/all_to_all | solution.py:99
  45.9 61.7 %copy-start.8 = (bf16[1,1,256,384]{3,2,1,0:T(8,128)(2,1)S(1)}, bf16[1,1,256,384]{3,2,1,0:T(8,128)(2,1)}, u32[]{:S(2)}) copy-start(bf16[1,1,256,384]{3,2,1,0:T(8,128)(2,1)} %param.20) | copy-start | bytes 589828
  45.9 61.9 %copy-start.7 = (bf16[1,1,256,384]{3,2,1,0:T(8,128)(2,1)S(1)}, bf16[1,1,256,384]{3,2,1,0:T(8,128)(2,1)}, u32[]{:S(2)}) copy-start(bf16[1,1,256,384]{3,2,1,0:T(8,128)(2,1)} %param.21) | copy-start | bytes 589828
  62.1 20.7 %all-to-all-start.3 = ((bf16[1,1,2,40,8,384]{5,3,2,1,0,4:T(8,128)(2,1)}), bf16[1,1,2,40,8,384]{5,3,2,1,0,4:T(8,128)(2,1)S(1)}, u32[]{:S(2)}, u32[]{:S(2)}) async-start(bf16[1,1,2,40,8,384]{5,3,2,1,0,4:T(8,128)(2,1)} %copy.71), calls=%async_computation.3 | async-start | bytes 983040 | tf_op jit(solution)/shard_map/all_to_all | solution.py:106
  82.8 20.7 %all-to-all-start.5 = ((bf16[1,1,2,40,8,384]{5,3,2,1,0,4:T(8,128)(2,1)}), bf16[1,1,2,40,8,384]{5,3,2,1,0,4:T(8,128)(2,1)S(1)}, u32[]{:S(2)}, u32[]{:S(2)}) async-start(bf16[1,1,2,40,8,384]{5,3,2,1,0,4:T(8,128)(2,1)} %copy.75), calls=%async_computation.5 | async-start | bytes 983040 | tf_op jit(solution)/shard_map/all_to_all | solution.py:113
  103.4 20.7 %all-to-all-start.7 = ((bf16[1,1,2,40,8,384]{5,3,2,1,0,4:T(8,128)(2,1)}), bf16[1,1,2,40,8,384]{5,3,2,1,0,4:T(8,128)(2,1)S(1)}, u32[]{:S(2)}, u32[]{:S(2)}) async-start(bf16[1,1,2,40,8,384]{5,3,2,1,0,4:T(8,128)(2,1)} %copy.79), calls=%async_computation.7 | async-start | bytes 983040 | tf_op jit(solution)/shard_map/all_to_all | solution.py:120
  130.1 3.1 %copy-start.9 = (bf16[640,3,128]{2,1,0:T(4,128)(2,1)S(1)}, bf16[640,3,128]{2,1,0:T(4,128)(2,1)}, u32[]{:S(2)}) copy-start(bf16[640,3,128]{2,1,0:T(4,128)(2,1)} %reshape.393) | copy-start | bytes 1474564
  137.5 19.3 %copy-start.14 = (f32[1,40,64]{2,1,0:T(8,128)S(1)}, f32[1,40,64]{2,1,0:T(8,128)}, u32[]{:S(2)}) copy-start(f32[1,40,64]{2,1,0:T(8,128)} %param.24) | copy-start | bytes 30724
  137.5 19.4 %copy-start.13 = (bf16[1,384,64]{1,2,0:T(8,128)(2,1)S(1)}, bf16[1,384,64]{1,2,0:T(8,128)(2,1)}, u32[]{:S(2)}) copy-start(bf16[1,384,64]{1,2,0:T(8,128)(2,1)} %param.25) | copy-start | bytes 147460
  142.7 41.0 %all-to-all-start.9 = ((bf16[2,8,1,40,1,384]{5,3,0,4,2,1:T(8,128)(2,1)}), bf16[2,8,1,40,1,384]{5,3,0,4,2,1:T(8,128)(2,1)S(1)}, u32[]{:S(2)}, u32[]{:S(2)}) async-start(bf16[2,8,1,40,1,384]{5,3,0,4,2,1:T(8,128)(2,1)} %copy.87), calls=%async_computation.9 | async-start | bytes 983040 | tf_op jit(solution)/shard_map/all_to_all | solution.py:146
  146.3 47.2 %collective-permute-start.1 = (bf16[256,384]{1,0:T(8,128)(2,1)S(1)}, bf16[256,384]{1,0:T(8,128)(2,1)S(1)}, u32[]{:S(2)}, u32[]{:S(2)}) collective-permute-start(bf16[256,384]{1,0:T(8,128)(2,1)S(1)} %get-tuple-element.35), channel_id=1, source_target_pairs={{0,256},{256,0},{1,257},{257,1},{2,258},{258,2},{3,259},{259,3},{4... | collective-permute-start | bytes 589832 | tf_op jit(solution)/shard_map/ppermute | solution.py:21
  154.0 39.5 %collective-permute-start.2 = (bf16[256,384]{1,0:T(8,128)(2,1)S(1)}, bf16[256,384]{1,0:T(8,128)(2,1)S(1)}, u32[]{:S(2)}, u32[]{:S(2)}) collective-permute-start(bf16[256,384]{1,0:T(8,128)(2,1)S(1)} %get-tuple-element.34), channel_id=1, source_target_pairs={{0,256},{256,0},{1,257},{257,1},{2,258},{258,2},{3,259},{259,3},{4... | collective-permute-start | bytes 589832 | tf_op jit(solution)/shard_map/ppermute | solution.py:21
  185.7 9.5 %collective-permute-start = (bf16[40,64]{0,1:T(8,128)(2,1)S(1)}, bf16[40,64]{0,1:T(8,128)(2,1)S(1)}, u32[]{:S(2)}, u32[]{:S(2)}) collective-permute-start(bf16[40,64]{0,1:T(8,128)(2,1)S(1)} %get-tuple-element.30), channel_id=1, source_target_pairs={{0,256},{256,0},{1,257},{257,1},{2,258},{258,2},{3,259},{259,3},{4... | collective-permute-start | bytes 15368 | tf_op jit(solution)/shard_map/ppermute | solution.py:21
  (2 other events, 1.9 us)
where the time goes:
time: 199 us; the launch traced here: 197 us
  waiting for transfers between devices  65.7 us (33%)
  starting transfers between devices  48.8 us (25%)
  blocking collectives  39.2 us (20%)
  local copies, waits for them, and re-layouts  19.1 us (10%)
  matrix products  12.8 us (6%)
  other arithmetic  9.04 us (5%)
  between operations  2.61 us (1%)
    all_gather x1, blocking collectives, per_device(): lax.all_gather(head_weight[0], 'sp', axis=0, tiled=True).astype(jnp.float32)  26.7 us
    ppermute x3, starting transfers between devices, swapped(): return lax.ppermute(value, axis, pairs)  17.6 us
    all_to_all x1, waiting for transfers between devices, per_device(): lax.all_to_all(lax.all_to_all(split_heads(values[0]), 'cfg', split_axis=0...  16.3 us
    all_to_all x1, waiting for transfers between devices, per_device(): lax.all_to_all(lax.all_to_all(split_heads(key_rot), 'cfg', split_axis=0,...  16.3 us
    all_to_all x1, waiting for transfers between devices, per_device(): lax.all_to_all(lax.all_to_all(split_heads(query_rot), 'cfg', split_axis=0...  16.3 us
    all_to_all x1, waiting for transfers between devices, per_device(): lax.all_to_all(lax.all_to_all(split_heads(cross_norm), 'cfg', split_axis=...  14.9 us
    all_to_all x1, starting transfers between devices, per_device(): lax.all_to_all(lax.all_to_all(split_heads(query_rot), 'cfg', split_axis=0...  10.3 us
    unnamed x49, local copies, waits for them, and re-layouts  7.99 us
  transfers between devices with their start and end apart: 10, of which 6 were waited for; matrix products, arithmetic and copies ran while one was open for 5% of the time, Pallas kernels for 0%

commit v1 on v0

v1 whole, which is shorter than its diff:
```python
import math

import jax
import jax.numpy as jnp
from jax import lax
from jax.experimental import pallas as pl
from jax.experimental.pallas import tpu as pltpu
from jax.sharding import PartitionSpec as P

HEAD = 128
STEPS = 40
TIME_SHIFT = 12.0
HIGH_GUIDE = 4.0
LOW_GUIDE = 3.0
NORM_EPS = 1e-06

MESH = pl.DeviceIdType.MESH
BF16 = jnp.bfloat16
F32 = jnp.float32
RING = (4, 3, 5, 2, 6, 1, 7)
V, K, Q, C, R = range(5)


def sigma_at(index):
    frac = 1.0 - index / STEPS
    return TIME_SHIFT * frac / (1.0 + (TIME_SHIFT - 1.0) * frac)


def contract_last(a, b):
    return lax.dot_general(a, b, (((1,), (1,)), ((), ())), preferred_element_type=F32)


def body(n, rows, heads, *refs):
    (
        q_hbm, k_hbm, v_hbm, c_hbm, qg_hbm, kg_hbm, cg_hbm, tk_hbm, tv_hbm, len_hbm, step_hbm, lat_hbm, w_hbm,
        clean_out, hlat_out, hk_out, hv_out,
        q_in, k_in, c_in, qg, kg, cg, tk, tv, length, step, lat, w_in,
        q_src, k_src, c_src, v_dst, k_dst, q_dst, c_dst,
        kr, qr, cr, va, tva, self_o, hid, cos_t, sin_t,
        tk_m, tv_m, wcat, col_src, col_dst, p_src, p_dst, clean_v, step_v,
        load_sem, send_sem, recv_sem, col_send, col_recv, x_send, x_recv, out_sem,
    ) = refs
    local = heads // n
    width = local * HEAD
    e = lax.axis_index("expert")
    c = lax.axis_index("cfg")
    z = lax.axis_index("sp")

    def chip(d):
        return lax.rem(z + d, n)

    def core(x):
        return lax.rem(c + x, 2)

    remote = [(d, x) for d in RING for x in (0, 1)] + [(0, 1)]

    barrier = pltpu.get_barrier_semaphore()
    for d, x in remote:
        pl.semaphore_signal(barrier, 1, device_id={"cfg": core(x), "sp": chip(d)}, device_id_type=MESH)
    pl.semaphore_signal(barrier, 1, device_id={"expert": 1 - e}, device_id_type=MESH)

    loads = []
    for i, (src, dst) in enumerate(
        (
            (k_hbm.at[0], k_in), (kg_hbm, kg), (q_hbm.at[0], q_in), (qg_hbm, qg), (c_hbm.at[0], c_in), (cg_hbm, cg),
            (tk_hbm.at[0, 0], tk), (tv_hbm.at[0, 0], tv), (len_hbm, length), (step_hbm, step), (lat_hbm.at[0], lat),
            (w_hbm.at[0], w_in),
        )
    ):
        copy = pltpu.make_async_copy(src, dst, load_sem.at[i])
        copy.start()
        loads.append(copy)

    sends = []

    def move(a, d, x, src, dst):
        if (d, x) == (0, 0):
            copy = pltpu.make_async_copy(src, dst, recv_sem.at[a, 0, 0])
            copy.start()
            return
        copy = pltpu.make_async_remote_copy(
            src, dst, send_sem.at[a, d, x], recv_sem.at[a, d, x],
            device_id={"cfg": core(x), "sp": chip(d)}, device_id_type=MESH,
        )
        copy.start()
        sends.append(copy)

    def arrived(a, d, x, ref):
        pltpu.make_async_copy(ref, ref, recv_sem.at[a, d, x]).wait()

    def v_move(d, x):
        cols = pl.ds(pl.multiple_of(chip(d) * width, HEAD), width)
        move(V, d, x, v_hbm.at[0, core(x), :, cols], v_dst.at[z, c])

    v_move(0, 0)
    pl.semaphore_wait(barrier, len(remote) + 1)
    for d, x in remote:
        v_move(d, x)

    lane = lax.broadcasted_iota(jnp.int32, (rows, HEAD), 1)
    even = lax.rem(lane, 2) == 0
    row = lax.broadcasted_iota(jnp.int32, (rows, HEAD), 0)
    position = ((c * n + z) * rows + row).astype(F32)
    pair = (lane // 2).astype(F32)
    angle = position * jnp.exp(-(2.0 * pair / HEAD) * math.log(10000.0))
    cos_t[...] = jnp.cos(angle)
    sin = jnp.sin(angle)
    sin_t[...] = jnp.where(even, -sin, sin)

    def prepare(x_ref, g_ref, o_ref, rope):
        for b in range(2):

            def square(i, total):
                for j in range(local):
                    cols = pl.ds(pl.multiple_of(i * width + j * HEAD, HEAD), HEAD)
                    x = x_ref[b, :, cols].astype(F32)
                    total = total + x * x
                return total

            total = lax.fori_loop(0, n, square, jnp.zeros((rows, HEAD), F32))
            scale = lax.rsqrt(jnp.sum(total, axis=-1, keepdims=True) / (heads * HEAD) + NORM_EPS)

            def one(i, carry):
                for j in range(local):
                    cols = pl.ds(pl.multiple_of(i * width + j * HEAD, HEAD), HEAD)
                    x = x_ref[b, :, cols].astype(F32) * scale * g_ref[:, cols]
                    if rope:
                        partner = jnp.where(even, pltpu.roll(x, HEAD - 1, 1), pltpu.roll(x, 1, 1))
                        x = x * cos_t[...] + partner * sin_t[...]
                    o_ref[b, i * local + j] = x.astype(BF16)
                return carry

            lax.fori_loop(0, n, one, 0)

    def spread(a, src, dst):
        for d, x in [*remote, (0, 0)]:
            move(a, d, x, src.at[core(x), pl.ds(chip(d) * local, local)], dst.at[:, z, c])

    loads[0].wait()
    loads[1].wait()
    prepare(k_in, kg, k_src, True)
    spread(K, k_src, k_dst)
    loads[2].wait()
    loads[3].wait()
    prepare(q_in, qg, q_src, True)
    spread(Q, q_src, q_dst)
    loads[4].wait()
    loads[5].wait()
    prepare(c_in, cg, c_src, False)
    spread(C, c_src, c_dst)

    for i in range(6, 12):
        loads[i].wait()
    count = length[0, 0, 0]
    text = tk.shape[0]
    keep = lax.broadcasted_iota(jnp.int32, (text, width), 0) < count
    tk_m[...] = jnp.where(keep, tk[...].astype(F32), 0.0).astype(BF16)
    tv_m[...] = jnp.where(keep, tv[...].astype(F32), 0.0).astype(BF16)
    handed = []
    for i, (src, dst) in enumerate(((tk_m, hk_out.at[0, 0]), (tv_m, hv_out.at[0, 0]))):
        copy = pltpu.make_async_remote_copy(
            src, dst, x_send.at[i], x_recv.at[i], device_id={"expert": 1 - e}, device_id_type=MESH
        )
        copy.start()
        handed.append(copy)

    w = w_in[...].astype(F32)
    wcat[:, 0:HEAD] = jnp.concatenate([w, w], axis=1).astype(BF16)
    wcat[:, HEAD : 2 * HEAD] = jnp.ones((width, HEAD), BF16)
    col_src[...] = jnp.dot(jnp.ones((8, width), BF16), wcat[:, 0:HEAD], preferred_element_type=F32)
    col_dst[z] = col_src[...]
    for d in RING:
        copy = pltpu.make_async_remote_copy(
            col_src, col_dst.at[z], col_send.at[d], col_recv.at[d], device_id={"sp": chip(d)}, device_id_type=MESH
        )
        copy.start()
        sends.append(copy)

    for h in range(local):
        tva[h, :, 0:HEAD] = tv[:, h * HEAD : (h + 1) * HEAD]
        tva[h, :, HEAD : 2 * HEAD] = jnp.ones((text, HEAD), BF16)
        va[h, :, HEAD : 2 * HEAD] = jnp.ones((va.shape[1], HEAD), BF16)

    everyone = [(d, x) for d in (0, *RING) for x in (0, 1)]
    pair_rows = 2 * rows

    for d, x in everyone:
        arrived(V, d, x, v_dst.at[chip(n - d), core(x)])
    for s in range(n):
        for h in range(local):
            block = v_dst[s, :, :, h * HEAD : (h + 1) * HEAD].astype(F32)
            va[h, s * pair_rows : (s + 1) * pair_rows, 0:HEAD] = block.reshape(pair_rows, HEAD).astype(BF16)

    def gather(a, dst, out):
        for d, x in everyone:
            arrived(a, d, x, dst.at[:, chip(n - d), core(x)])
        for h in range(local):
            for s in range(n):
                block = dst[h, s].astype(F32)
                out[h, s * pair_rows : (s + 1) * pair_rows, :] = block.reshape(pair_rows, HEAD).astype(BF16)

    gather(K, k_dst, kr)
    gather(Q, q_dst, qr)
    factor = math.log2(math.e) / math.sqrt(HEAD)
    step_rows = 2 * pair_rows
    blocks = n // 2
    for h in range(local):
        for r in range(blocks):
            part = slice(r * step_rows, (r + 1) * step_rows)
            s = contract_last(qr[h, part, :], kr[h])
            p = jnp.exp2((s - jnp.max(s, axis=-1, keepdims=True)) * factor).astype(BF16)
            o = jnp.dot(p, va[h], preferred_element_type=F32)
            self_o[h, part, :] = o[:, 0:HEAD] / o[:, HEAD : 2 * HEAD]

    gather(C, c_dst, cr)
    used = lax.broadcasted_iota(jnp.int32, (step_rows, text), 1) < count
    out_lane = lax.broadcasted_iota(jnp.int32, (step_rows, HEAD), 1)
    half = HEAD // 2
    order = (4, 3, 5, 2, 6, 1, 7, 0)
    for r in range(blocks):
        pair_of = order[2 * r : 2 * r + 2]
        starts = [pl.multiple_of(chip(d) * pair_rows, pair_rows) for d in pair_of]

        def take(ref, h):
            return jnp.concatenate([ref[h, pl.ds(start, pair_rows), :] for start in starts], axis=0)

        for h in range(local):
            s = contract_last(take(cr, h), tk[:, h * HEAD : (h + 1) * HEAD])
            s = jnp.where(used, s, -jnp.inf)
            p = jnp.exp2((s - jnp.max(s, axis=-1, keepdims=True)) * factor).astype(BF16)
            o = jnp.dot(p, tva[h], preferred_element_type=F32)
            hid[:, h * HEAD : (h + 1) * HEAD] = (take(self_o, h) + o[:, 0:HEAD] / o[:, HEAD : 2 * HEAD]).astype(BF16)
        both = jnp.dot(hid[...], wcat[...], preferred_element_type=F32)
        mean = both[:, HEAD : 2 * HEAD] / width
        square = jnp.zeros((step_rows, HEAD), F32)
        for h in range(local):
            centred = hid[:, h * HEAD : (h + 1) * HEAD].astype(F32) - mean
            square = square + centred * centred
        spread2 = jnp.broadcast_to(jnp.sum(square, axis=-1, keepdims=True), (step_rows, HEAD))
        partial = both[:, 0:HEAD] - mean * col_src[0:1, :]

        def parts(x, count):
            out = []
            for _ in range(count):
                out.append(x.astype(BF16).astype(F32))
                x = x - out[-1]
            return out

        hi, lo = parts(partial, 2)
        sent = jnp.where(out_lane < half, hi, lo)
        for i, stat in enumerate((*parts(mean, 3), *parts(spread2, 2))):
            sent = jnp.where(out_lane == HEAD - 5 + i, stat, sent)
        for i, d in enumerate(pair_of):
            block = sent[i * pair_rows : (i + 1) * pair_rows].reshape(2, rows, HEAD)
            p_src[d] = block.astype(BF16)
            for x in (0, 1):
                move(R, d, x, p_src.at[d, core(x)], p_dst.at[c, z])

    for d in RING:
        arrived_col = pltpu.make_async_copy(col_src, col_dst.at[chip(n - d)], col_recv.at[d])
        arrived_col.wait()
    for d, x in everyone:
        arrived(R, d, x, p_dst.at[core(x), chip(n - d)])
    pick_row = lax.broadcasted_iota(jnp.int32, (HEAD, HEAD), 0)
    pick_col = lax.broadcasted_iota(jnp.int32, (HEAD, HEAD), 1)
    in_sum = (pick_row < HEAD - 5) & (lax.rem(pick_row, half) == lax.rem(pick_col, half))
    in_mean = (pick_row >= HEAD - 5) & (pick_row < HEAD - 2)
    in_square = pick_row >= HEAD - 2
    picks = [jnp.where(m, 1.0, 0.0).astype(BF16) for m in (in_sum, in_mean, in_square)]
    velocity = []
    for b in range(2):
        got = p_dst[b].astype(F32).reshape(n * rows, HEAD).astype(BF16)
        sums, means, squares = [
            jnp.dot(got, m, preferred_element_type=F32).reshape(n, rows, HEAD) for m in picks
        ]
        mean = jnp.sum(means, axis=0) / n
        away = means - mean[None]
        variance = (jnp.sum(squares, axis=0) + width * jnp.sum(away * away, axis=0)) / (heads * HEAD)
        total = jnp.zeros((rows, HEAD), F32)
        for s in range(n):
            total = total + (sums[s] + away[s] * col_dst[s, 0:1, :])
        velocity.append(total * lax.rsqrt(variance + NORM_EPS))
    guide = jnp.where(e == 0, HIGH_GUIDE, LOW_GUIDE)
    guided = (velocity[1] + guide * (velocity[0] - velocity[1]))[:, 0:half]
    now = jnp.full((rows, half), step[0, 0], jnp.int32).astype(F32)
    sigma_now = sigma_at(now)
    sigma_next = sigma_at(now + 1.0)
    step_v[...] = (lat[...] + (sigma_next - sigma_now) * guided).astype(BF16)
    copy = pltpu.make_async_remote_copy(
        step_v, hlat_out.at[0], x_send.at[2], x_recv.at[2], device_id={"expert": 1 - e}, device_id_type=MESH
    )
    copy.start()
    handed.append(copy)
    clean_v[...] = lat[...] - sigma_now * guided
    done = pltpu.make_async_copy(clean_v, clean_out.at[0], out_sem)
    done.start()
    for copy in sends:
        copy.wait_send()
    done.wait()
    for copy in handed:
        copy.wait()


def per_device(n, *args):
    queries, text_keys, latent, head_weight = args[0], args[7], args[11], args[12]
    rows, features = queries.shape[2:]
    heads = features // HEAD
    local = heads // n
    text, width = text_keys.shape[2:]
    channels = latent.shape[2]
    tokens = 2 * n * rows

    def kernel(*refs):
        body(n, rows, heads, *refs)

    anywhere = pl.BlockSpec(memory_space=pl.ANY)
    raw = pltpu.VMEM((2, rows, features), BF16)
    gain = pltpu.VMEM((1, features), F32)
    source = pltpu.VMEM((2, heads, rows, HEAD), BF16)
    landed = pltpu.VMEM((local, n, 2, rows, HEAD), BF16)
    merged = pltpu.VMEM((local, tokens, HEAD), BF16)
    dma = pltpu.SemaphoreType.DMA
    return pl.pallas_call(
        kernel,
        out_shape=(
            jax.ShapeDtypeStruct(latent.shape, F32),
            jax.ShapeDtypeStruct(latent.shape, BF16),
            jax.ShapeDtypeStruct(text_keys.shape, BF16),
            jax.ShapeDtypeStruct(text_keys.shape, BF16),
        ),
        in_specs=[anywhere] * len(args),
        out_specs=(anywhere,) * 4,
        scratch_shapes=[
            raw, raw, raw, gain, gain, gain,
            pltpu.VMEM((text, width), BF16), pltpu.VMEM((text, width), BF16),
            pltpu.SMEM((1, 1, 1), jnp.int32), pltpu.SMEM((1, 1), jnp.int32),
            pltpu.VMEM((rows, channels), F32), pltpu.VMEM((width, channels), BF16),
            source, source, source,
            pltpu.VMEM((n, 2, rows, width), BF16), landed, landed, landed,
            merged, merged, merged,
            pltpu.VMEM((local, tokens, 2 * HEAD), BF16), pltpu.VMEM((local, text, 2 * HEAD), BF16),
            pltpu.VMEM((local, tokens, HEAD), F32), pltpu.VMEM((4 * rows, width), BF16),
            pltpu.VMEM((rows, HEAD), F32), pltpu.VMEM((rows, HEAD), F32),
            pltpu.VMEM((text, width), BF16), pltpu.VMEM((text, width), BF16),
            pltpu.VMEM((width, 2 * HEAD), BF16), pltpu.VMEM((8, HEAD), F32), pltpu.VMEM((n, 8, HEAD), F32),
            pltpu.VMEM((n, 2, rows, HEAD), BF16), pltpu.VMEM((2, n, rows, HEAD), BF16),
            pltpu.VMEM((rows, channels), F32), pltpu.VMEM((rows, channels), BF16),
            dma((12,)), dma((5, n, 2)), dma((5, n, 2)), dma((n,)), dma((n,)), dma((3,)), dma((3,)), dma,
        ],
        compiler_params=pltpu.CompilerParams(
            collective_id=0, has_side_effects=True, vmem_limit_bytes=60 * 1024 * 1024
        ),
        cost_estimate=pl.CostEstimate(
            flops=1_000_000_000, bytes_accessed=4_000_000, transcendentals=2_000_000
        ),
    )(*args)


def solution(mesh):
    token_spec = P("expert", None, ("rep", "cfg", "sp"), None)
    text_spec = P("expert", "cfg", "rep", "sp")
    latent_spec = P("expert", ("rep", "cfg", "sp"), None)
    gain_spec = P("expert", None)
    in_specs = (
        *(token_spec,) * 4,
        *(gain_spec,) * 3,
        text_spec,
        text_spec,
        P("expert", "cfg", "rep"),
        P("expert", "rep"),
        latent_spec,
        P("expert", "sp", None),
    )
    out_specs = (latent_spec, latent_spec, text_spec, text_spec)
    count = mesh.shape["sp"]

    def run(*args):
        return per_device(count, *args)

    return jax.shard_map(run, mesh=mesh, in_specs=in_specs, out_specs=out_specs, check_vma=False)
```

time: 199 us -> 80.4 us (0.40)
  Pallas kernels: 0 us -> 72.4 us
  waiting for transfers between devices: 65.7 us -> 0 us
  starting transfers between devices: 48.8 us -> 0 us
  blocking collectives: 39.2 us -> 0 us
  local copies, waits for them, and re-layouts: 19.1 us -> 5.83 us
  matrix products: 12.8 us -> 0 us
  other arithmetic: 9.04 us -> 0 us
    pallas_call x0 -> x1, Pallas kernels: none -> 72.4 us  [per_device(): pl.pallas_call(kernel, out_shape=(jax.ShapeDtypeStruct(latent.shape, F32)...]
    all_to_all x7 -> x0, waiting for transfers between devices: 64.7 us -> none  [the longest x1 16.3 us: per_device(): lax.all_to_all(lax.all_to_all(split_heads(values[0]), 'cfg', split_axis=0...]
    all_to_all x7 -> x0, starting transfers between devices: 31.2 us -> none  [the longest x1 10.3 us: per_device(): lax.all_to_all(lax.all_to_all(split_heads(query_rot), 'cfg', split_axis=0...]
    all_gather x1 -> x0, blocking collectives: 26.7 us -> none  [per_device(): lax.all_gather(head_weight[0], 'sp', axis=0, tiled=True).astype(jnp.float32)]
    ppermute x3 -> x0, starting transfers between devices: 17.6 us -> none  [swapped(): return lax.ppermute(value, axis, pairs)]
    all_to_all x3 -> x0, blocking collectives: 12.5 us -> none  [the longest x1 4.29 us: per_device(): lax.all_to_all(hidden.reshape(1, sp_count, 2, tok_rows, 1, local_width),...]
    sub x2 -> x0, matrix products: 7.08 us -> none  [attend_block(): exponent = jnp.exp(scores - row_max)]
    dot_general x3 -> x0, matrix products: 5.75 us -> none  [the longest x2 5.01 us: attend_block(): jnp.einsum('hqk,khd->qhd', weights, value_heads, preferred_element_type=j...]
  transfers between devices with their start and end apart: 10 -> 0, of which waited for: 6 -> 0; matrix products, arithmetic and copies ran while one was open for 5% -> 0% of each run, Pallas kernels for 0% -> 0%
where the time goes in v1:
time: 80.4 us; the launch traced here: 80.2 us
  Pallas kernels  72.4 us (90%)
  local copies, waits for them, and re-layouts  5.83 us (7%)
  between operations  1.94 us (2%)
    pallas_call x1, Pallas kernels, per_device(): pl.pallas_call(kernel, out_shape=(jax.ShapeDtypeStruct(latent.shape, F32)...  72.4 us
    unnamed x9, local copies, waits for them, and re-layouts  5.83 us

profile of v1, /device:TPU:6, one launch (start us, length us, event | category | flops | bytes accessed | tf_op | source)
XLA Modules:
  0.0 80.2 jit_solution(12524895367210408571)
XLA Ops:
  1.9 1.5 %copy.17.refs_12_ = bf16[1,384,64]{2,1,0:T(8,128)(2,1)} copy(bf16[1,384,64]{1,2,0:T(8,128)(2,1)} %param.25) | data formatting | bytes 98304 | tf_op args[12]
  3.5 72.4 %shard_map.156 = (f32[1,40,64]{2,1,0:T(8,128)}, bf16[1,40,64]{2,1,0:T(8,128)(2,1)}, bf16[1,1,256,384]{3,2,1,0:T(8,128)(2,1)}, bf16[1,1,256,384]{3,2,1,0:T(8,128)(2,1)}) custom-call(bf16[1,2,40,3072]{3,2,1,0:T(8,128)(2,1)} %refs_0_.1, bf16[1,2,40,3072]{3,2,1,0:T(8,128)(2,1)} %refs_1_.1, bf16[1,2,40,3072]{3,2,1,0:T(8,128)(2,1)} %refs_2_.1, ...), custom_call_target="tpu_custom_call" | custom-call | flops 1000000000 | bytes 4000000 | tf_op jit(solution)/shard_map/pallas_call | solution.py:323
  75.9 0.0 copy-start.1
  75.9 1.3 %copy.24 = f32[1,40,64]{2,1,0:T(8,128)} copy(f32[1,40,64]{2,1,0:T(8,128)} %get-tuple-element.8) | data formatting | bytes 20480
  77.2 0.0 copy-done.1
  77.2 0.6 copy.25
  77.8 0.0 copy-start
  77.8 1.7 %copy.26 = bf16[1,1,256,384]{3,2,1,0:T(8,128)(2,1)} copy(bf16[1,1,256,384]{3,2,1,0:T(8,128)(2,1)} %get-tuple-element.10) | data formatting | bytes 393216
  79.5 0.0 copy-done
  79.5 0.7 copy.27
Async XLA Ops:
  75.9 1.4 %copy-start.1 = (bf16[1,40,64]{2,1,0:T(8,128)(2,1)S(1)}, bf16[1,40,64]{2,1,0:T(8,128)(2,1)}, u32[]{:S(2)}) copy-start(bf16[1,40,64]{2,1,0:T(8,128)(2,1)} %get-tuple-element.9) | copy-start | bytes 15364
  77.8 1.7 %copy-start = (bf16[1,1,256,384]{3,2,1,0:T(8,128)(2,1)S(1)}, bf16[1,1,256,384]{3,2,1,0:T(8,128)(2,1)}, u32[]{:S(2)}) copy-start(bf16[1,1,256,384]{3,2,1,0:T(8,128)(2,1)} %get-tuple-element.11) | copy-start | bytes 589828

commit v2 on v1

--- a/solution.py
+++ b/solution.py
@@ -36,7 +36,7 @@
         clean_out, hlat_out, hk_out, hv_out,
         q_in, k_in, c_in, qg, kg, cg, tk, tv, length, step, lat, w_in,
         q_src, k_src, c_src, v_dst, k_dst, q_dst, c_dst,
-        kr, qr, cr, va, tva, self_o, hid, cos_t, sin_t,
+        kr, qr, cr, vr, self_o, hid, cos_t, sin_t,
         tk_m, tv_m, wcat, col_src, col_dst, p_src, p_dst, clean_v, step_v,
         load_sem, send_sem, recv_sem, col_send, col_recv, x_send, x_recv, out_sem,
     ) = refs
@@ -164,10 +164,11 @@
         copy.start()
         handed.append(copy)
 
-    w = w_in[...].astype(F32)
-    wcat[:, 0:HEAD] = jnp.concatenate([w, w], axis=1).astype(BF16)
-    wcat[:, HEAD : 2 * HEAD] = jnp.ones((width, HEAD), BF16)
-    col_src[...] = jnp.dot(jnp.ones((8, width), BF16), wcat[:, 0:HEAD], preferred_element_type=F32)
+    half = HEAD // 2
+    wcat[0:half, :] = w_in[...]
+    wcat[half:HEAD, :] = w_in[...]
+    wcat[HEAD : 2 * HEAD, :] = jnp.ones((HEAD, width), BF16)
+    col_src[...] = contract_last(jnp.ones((8, width), BF16), wcat[0:HEAD, :])
     col_dst[z] = col_src[...]
     for d in RING:
         copy = pltpu.make_async_remote_copy(
@@ -176,50 +177,46 @@
         copy.start()
         sends.append(copy)
 
-    for h in range(local):
-        tva[h, :, 0:HEAD] = tv[:, h * HEAD : (h + 1) * HEAD]
-        tva[h, :, HEAD : 2 * HEAD] = jnp.ones((text, HEAD), BF16)
-        va[h, :, HEAD : 2 * HEAD] = jnp.ones((va.shape[1], HEAD), BF16)
-
     everyone = [(d, x) for d in (0, *RING) for x in (0, 1)]
     pair_rows = 2 * rows
 
-    for d, x in everyone:
-        arrived(V, d, x, v_dst.at[chip(n - d), core(x)])
-    for s in range(n):
+    def start_of(d):
+        return pl.multiple_of(chip(n - d) * pair_rows, pair_rows)
+
+    def gather(a, dst, out, d):
+        at = chip(n - d)
+        for x in (0, 1):
+            arrived(a, d, x, dst.at[at, core(x)] if a == V else dst.at[:, at, core(x)])
         for h in range(local):
-            block = v_dst[s, :, :, h * HEAD : (h + 1) * HEAD].astype(F32)
-            va[h, s * pair_rows : (s + 1) * pair_rows, 0:HEAD] = block.reshape(pair_rows, HEAD).astype(BF16)
-
-    def gather(a, dst, out):
-        for d, x in everyone:
-            arrived(a, d, x, dst.at[:, chip(n - d), core(x)])
-        for h in range(local):
-            for s in range(n):
-                block = dst[h, s].astype(F32)
-                out[h, s * pair_rows : (s + 1) * pair_rows, :] = block.reshape(pair_rows, HEAD).astype(BF16)
-
-    gather(K, k_dst, kr)
-    gather(Q, q_dst, qr)
+            block = dst[at, :, :, h * HEAD : (h + 1) * HEAD] if a == V else dst[h, at]
+            block = block.astype(F32).reshape(pair_rows, HEAD).astype(BF16)
+            out[h, pl.ds(start_of(d), pair_rows), :] = block
+
     factor = math.log2(math.e) / math.sqrt(HEAD)
+
+    def weights(s):
+        exponent = jnp.exp2((s - jnp.max(s, axis=-1, keepdims=True)) * factor)
+        return (exponent * (1.0 / jnp.sum(exponent, axis=-1, keepdims=True))).astype(BF16)
+
+    for a, dst, out in ((V, v_dst, vr), (K, k_dst, kr), (Q, q_dst, qr)):
+        for d in (0, *RING):
+            gather(a, dst, out, d)
     step_rows = 2 * pair_rows
     blocks = n // 2
     for h in range(local):
         for r in range(blocks):
             part = slice(r * step_rows, (r + 1) * step_rows)
-            s = contract_last(qr[h, part, :], kr[h])
-            p = jnp.exp2((s - jnp.max(s, axis=-1, keepdims=True)) * factor).astype(BF16)
-            o = jnp.dot(p, va[h], preferred_element_type=F32)
-            self_o[h, part, :] = o[:, 0:HEAD] / o[:, HEAD : 2 * HEAD]
-
-    gather(C, c_dst, cr)
+            p = weights(contract_last(qr[h, part, :], kr[h]))
+            self_o[h, part, :] = jnp.dot(p, vr[h], preferred_element_type=F32)
+
     used = lax.broadcasted_iota(jnp.int32, (step_rows, text), 1) < count
     out_lane = lax.broadcasted_iota(jnp.int32, (step_rows, HEAD), 1)
-    half = HEAD // 2
-    order = (4, 3, 5, 2, 6, 1, 7, 0)
+    order = (0, *RING)
     for r in range(blocks):
         pair_of = order[2 * r : 2 * r + 2]
-        starts = [pl.multiple_of(chip(d) * pair_rows, pair_rows) for d in pair_of]
+        for d in pair_of:
+            gather(C, c_dst, cr, d)
+        starts = [start_of(d) for d in pair_of]
 
         def take(ref, h):
             return jnp.concatenate([ref[h, pl.ds(start, pair_rows), :] for start in starts], axis=0)
@@ -227,10 +224,9 @@
         for h in range(local):
             s = contract_last(take(cr, h), tk[:, h * HEAD : (h + 1) * HEAD])
             s = jnp.where(used, s, -jnp.inf)
-            p = jnp.exp2((s - jnp.max(s, axis=-1, keepdims=True)) * factor).astype(BF16)
-            o = jnp.dot(p, tva[h], preferred_element_type=F32)
-            hid[:, h * HEAD : (h + 1) * HEAD] = (take(self_o, h) + o[:, 0:HEAD] / o[:, HEAD : 2 * HEAD]).astype(BF16)
-        both = jnp.dot(hid[...], wcat[...], preferred_element_type=F32)
+            o = jnp.dot(weights(s), tv[:, h * HEAD : (h + 1) * HEAD], preferred_element_type=F32)
+            hid[:, h * HEAD : (h + 1) * HEAD] = (take(self_o, h) + o).astype(BF16)
+        both = contract_last(hid[...], wcat[...])
         mean = both[:, HEAD : 2 * HEAD] / width
         square = jnp.zeros((step_rows, HEAD), F32)
         for h in range(local):
@@ -250,7 +246,7 @@
         sent = jnp.where(out_lane < half, hi, lo)
         for i, stat in enumerate((*parts(mean, 3), *parts(spread2, 2))):
             sent = jnp.where(out_lane == HEAD - 5 + i, stat, sent)
-        for i, d in enumerate(pair_of):
+        for i, d in enumerate([(n - d) % n for d in pair_of]):
             block = sent[i * pair_rows : (i + 1) * pair_rows].reshape(2, rows, HEAD)
             p_src[d] = block.astype(BF16)
             for x in (0, 1):
@@ -301,8 +297,22 @@
         copy.wait()
 
 
+def hand_on(*refs):
+    sem = refs[-1]
+    arrive = [pltpu.make_async_copy(refs[i], refs[8 + i], sem.at[0, i]) for i in range(4)]
+    leave = [pltpu.make_async_copy(refs[8 + i], refs[4 + i], sem.at[1, i]) for i in range(4)]
+    for copy in arrive:
+        copy.start()
+    for i in range(4):
+        arrive[i].wait()
+        leave[i].start()
+    for copy in leave:
+        copy.wait()
+
+
 def per_device(n, *args):
-    queries, text_keys, latent, head_weight = args[0], args[7], args[11], args[12]
+    queries, text_keys, latent = args[0], args[7], args[11]
+    args = (*args[:12], jnp.swapaxes(args[12], 1, 2))
     rows, features = queries.shape[2:]
     heads = features // HEAD
     local = heads // n
@@ -320,7 +330,7 @@
     landed = pltpu.VMEM((local, n, 2, rows, HEAD), BF16)
     merged = pltpu.VMEM((local, tokens, HEAD), BF16)
     dma = pltpu.SemaphoreType.DMA
-    return pl.pallas_call(
+    results = pl.pallas_call(
         kernel,
         out_shape=(
             jax.ShapeDtypeStruct(latent.shape, F32),
@@ -334,15 +344,14 @@
             raw, raw, raw, gain, gain, gain,
             pltpu.VMEM((text, width), BF16), pltpu.VMEM((text, width), BF16),
             pltpu.SMEM((1, 1, 1), jnp.int32), pltpu.SMEM((1, 1), jnp.int32),
-            pltpu.VMEM((rows, channels), F32), pltpu.VMEM((width, channels), BF16),
+            pltpu.VMEM((rows, channels), F32), pltpu.VMEM((channels, width), BF16),
             source, source, source,
             pltpu.VMEM((n, 2, rows, width), BF16), landed, landed, landed,
-            merged, merged, merged,
-            pltpu.VMEM((local, tokens, 2 * HEAD), BF16), pltpu.VMEM((local, text, 2 * HEAD), BF16),
+            merged, merged, merged, merged,
             pltpu.VMEM((local, tokens, HEAD), F32), pltpu.VMEM((4 * rows, width), BF16),
             pltpu.VMEM((rows, HEAD), F32), pltpu.VMEM((rows, HEAD), F32),
             pltpu.VMEM((text, width), BF16), pltpu.VMEM((text, width), BF16),
-            pltpu.VMEM((width, 2 * HEAD), BF16), pltpu.VMEM((8, HEAD), F32), pltpu.VMEM((n, 8, HEAD), F32),
+            pltpu.VMEM((2 * HEAD, width), BF16), pltpu.VMEM((8, HEAD), F32), pltpu.VMEM((n, 8, HEAD), F32),
             pltpu.VMEM((n, 2, rows, HEAD), BF16), pltpu.VMEM((2, n, rows, HEAD), BF16),
             pltpu.VMEM((rows, channels), F32), pltpu.VMEM((rows, channels), BF16),
             dma((12,)), dma((5, n, 2)), dma((5, n, 2)), dma((n,)), dma((n,)), dma((3,)), dma((3,)), dma,
@@ -354,6 +363,14 @@
             flops=1_000_000_000, bytes_accessed=4_000_000, transcendentals=2_000_000
         ),
     )(*args)
+    return pl.pallas_call(
+        hand_on,
+        out_shape=tuple(jax.ShapeDtypeStruct(r.shape, r.dtype) for r in results),
+        in_specs=[anywhere] * 4,
+        out_specs=(anywhere,) * 4,
+        scratch_shapes=[*(pltpu.VMEM(r.shape, r.dtype) for r in results), dma((2, 4))],
+        compiler_params=pltpu.CompilerParams(vmem_limit_bytes=60 * 1024 * 1024),
+    )(*results)
 
 
 def solution(mesh):

time: 80.4 us -> 73.7 us (0.917)
  local copies, waits for them, and re-layouts: 5.83 us -> 0 us
  Pallas kernels: 72.4 us -> 71.4 us
    unnamed x9 -> x0, local copies, waits for them, and re-layouts: 5.83 us -> none
    pallas_call x1, Pallas kernels: 72.4 us -> 69.6 us  [per_device(): pl.pallas_call(kernel, out_shape=(jax.ShapeDtypeStruct(latent.shape, F32)...]
    pallas_call x0 -> x1, Pallas kernels: none -> 1.8 us  [per_device(): pl.pallas_call(hand_on, out_shape=tuple((jax.ShapeDtypeStruct(r.shape, r....]
where the time goes in v2:
time: 73.7 us; the launch traced here: 73.3 us
  Pallas kernels  71.4 us (97%)
  between operations  1.93 us (3%)
    pallas_call x1, Pallas kernels, per_device(): pl.pallas_call(kernel, out_shape=(jax.ShapeDtypeStruct(latent.shape, F32)...  69.6 us
    pallas_call x1, Pallas kernels, per_device(): pl.pallas_call(hand_on, out_shape=tuple((jax.ShapeDtypeStruct(r.shape, r....  1.8 us

profile of v2, /device:TPU:6, one launch (start us, length us, event | category | flops | bytes accessed | tf_op | source)
XLA Modules:
  0.0 73.3 jit_solution(14254264351572777807)
XLA Ops:
  1.9 69.6 %shard_map.156 = (f32[1,40,64]{2,1,0:T(8,128)}, bf16[1,40,64]{2,1,0:T(8,128)(2,1)}, bf16[1,1,256,384]{3,2,1,0:T(8,128)(2,1)}, bf16[1,1,256,384]{3,2,1,0:T(8,128)(2,1)}) custom-call(bf16[1,2,40,3072]{3,2,1,0:T(8,128)(2,1)} %refs_0_.1, bf16[1,2,40,3072]{3,2,1,0:T(8,128)(2,1)} %refs_1_.1, bf16[1,2,40,3072]{3,2,1,0:T(8,128)(2,1)} %refs_2_.1, ...), custom_call_target="tpu_custom_call" | custom-call | flops 1000000000 | bytes 4000000 | tf_op jit(solution)/shard_map/pallas_call | solution.py:333
  71.5 1.8 %shard_map.157 = (f32[1,40,64]{2,1,0:T(8,128)}, bf16[1,40,64]{2,1,0:T(8,128)(2,1)}, bf16[1,1,256,384]{3,2,1,0:T(8,128)(2,1)}, bf16[1,1,256,384]{3,2,1,0:T(8,128)(2,1)}) custom-call(f32[1,40,64]{2,1,0:T(8,128)} %get-tuple-element.8.refs_0_, bf16[1,40,64]{2,1,0:T(8,128)(2,1)} %get-tuple-element.9.refs_1_, bf16[1,1,256,384]{3,2,1,0:T(8,128)(2,1)} %get-tuple-element.10.refs_2_, ...), custom_call_target="tpu_custom_call" | custom-call | tf_op jit(solution)/shard_map/pallas_call | solution.py:366

commit v3 on v2

--- a/solution.py
+++ b/solution.py
@@ -168,7 +168,7 @@
     wcat[0:half, :] = w_in[...]
     wcat[half:HEAD, :] = w_in[...]
     wcat[HEAD : 2 * HEAD, :] = jnp.ones((HEAD, width), BF16)
-    col_src[...] = contract_last(jnp.ones((8, width), BF16), wcat[0:HEAD, :])
+    col_src[...] = contract_last(jnp.ones((8, width), BF16), wcat[0:HEAD, :])[0:1]
     col_dst[z] = col_src[...]
     for d in RING:
         copy = pltpu.make_async_remote_copy(
@@ -351,7 +351,7 @@
             pltpu.VMEM((local, tokens, HEAD), F32), pltpu.VMEM((4 * rows, width), BF16),
             pltpu.VMEM((rows, HEAD), F32), pltpu.VMEM((rows, HEAD), F32),
             pltpu.VMEM((text, width), BF16), pltpu.VMEM((text, width), BF16),
-            pltpu.VMEM((2 * HEAD, width), BF16), pltpu.VMEM((8, HEAD), F32), pltpu.VMEM((n, 8, HEAD), F32),
+            pltpu.VMEM((2 * HEAD, width), BF16), pltpu.VMEM((1, HEAD), F32), pltpu.VMEM((n, 1, HEAD), F32),
             pltpu.VMEM((n, 2, rows, HEAD), BF16), pltpu.VMEM((2, n, rows, HEAD), BF16),
             pltpu.VMEM((rows, channels), F32), pltpu.VMEM((rows, channels), BF16),
             dma((12,)), dma((5, n, 2)), dma((5, n, 2)), dma((n,)), dma((n,)), dma((3,)), dma((3,)), dma,

time: 73.7 us -> 73.5 us (level)
  no operation moved by 1% of the time
where the time goes in v3:
time: 73.5 us; the launch traced here: 73.2 us
  Pallas kernels  71.2 us (97%)
  between operations  1.93 us (3%)
    pallas_call x1, Pallas kernels, per_device(): pl.pallas_call(kernel, out_shape=(jax.ShapeDtypeStruct(latent.shape, F32)...  69.4 us
    pallas_call x1, Pallas kernels, per_device(): pl.pallas_call(hand_on, out_shape=tuple((jax.ShapeDtypeStruct(r.shape, r....  1.8 us

profile of v3, /device:TPU:6, one launch (start us, length us, event | category | flops | bytes accessed | tf_op | source)
XLA Modules:
  0.0 73.2 jit_solution(15613634992726972478)
XLA Ops:
  1.9 69.4 %shard_map.156 = (f32[1,40,64]{2,1,0:T(8,128)}, bf16[1,40,64]{2,1,0:T(8,128)(2,1)}, bf16[1,1,256,384]{3,2,1,0:T(8,128)(2,1)}, bf16[1,1,256,384]{3,2,1,0:T(8,128)(2,1)}) custom-call(bf16[1,2,40,3072]{3,2,1,0:T(8,128)(2,1)} %refs_0_.1, bf16[1,2,40,3072]{3,2,1,0:T(8,128)(2,1)} %refs_1_.1, bf16[1,2,40,3072]{3,2,1,0:T(8,128)(2,1)} %refs_2_.1, ...), custom_call_target="tpu_custom_call" | custom-call | flops 1000000000 | bytes 4000000 | tf_op jit(solution)/shard_map/pallas_call | solution.py:333
  71.4 1.8 %shard_map.157 = (f32[1,40,64]{2,1,0:T(8,128)}, bf16[1,40,64]{2,1,0:T(8,128)(2,1)}, bf16[1,1,256,384]{3,2,1,0:T(8,128)(2,1)}, bf16[1,1,256,384]{3,2,1,0:T(8,128)(2,1)}) custom-call(f32[1,40,64]{2,1,0:T(8,128)} %get-tuple-element.8.refs_0_, bf16[1,40,64]{2,1,0:T(8,128)(2,1)} %get-tuple-element.9.refs_1_, bf16[1,1,256,384]{3,2,1,0:T(8,128)(2,1)} %get-tuple-element.10.refs_2_, ...), custom_call_target="tpu_custom_call" | custom-call | tf_op jit(solution)/shard_map/pallas_call | solution.py:366

commit v4 on v3

--- a/solution.py
+++ b/solution.py
@@ -37,7 +37,7 @@
         q_in, k_in, c_in, qg, kg, cg, tk, tv, length, step, lat, w_in,
         q_src, k_src, c_src, v_dst, k_dst, q_dst, c_dst,
         kr, qr, cr, vr, self_o, hid, cos_t, sin_t,
-        tk_m, tv_m, wcat, col_src, col_dst, p_src, p_dst, clean_v, step_v,
+        tk_m, tv_m, wcat, col_src, col_dst, p_src, p_dst, pick_ref, sigmas, clean_v, step_v,
         load_sem, send_sem, recv_sem, col_send, col_recv, x_send, x_recv, out_sem,
     ) = refs
     local = heads // n
@@ -252,22 +252,30 @@
             for x in (0, 1):
                 move(R, d, x, p_src.at[d, core(x)], p_dst.at[c, z])
 
-    for d in RING:
-        arrived_col = pltpu.make_async_copy(col_src, col_dst.at[chip(n - d)], col_recv.at[d])
-        arrived_col.wait()
-    for d, x in everyone:
-        arrived(R, d, x, p_dst.at[core(x), chip(n - d)])
     pick_row = lax.broadcasted_iota(jnp.int32, (HEAD, HEAD), 0)
     pick_col = lax.broadcasted_iota(jnp.int32, (HEAD, HEAD), 1)
     in_sum = (pick_row < HEAD - 5) & (lax.rem(pick_row, half) == lax.rem(pick_col, half))
     in_mean = (pick_row >= HEAD - 5) & (pick_row < HEAD - 2)
     in_square = pick_row >= HEAD - 2
     picks = [jnp.where(m, 1.0, 0.0).astype(BF16) for m in (in_sum, in_mean, in_square)]
+    now = jnp.full((rows, half), step[0, 0], jnp.int32).astype(F32)
+    sigmas[0] = sigma_at(now)
+    sigmas[1] = sigma_at(now + 1.0)
+    for i, m in enumerate(picks):
+        pick_ref[i] = m
+    for copy in sends[: 4 * len(remote) + len(RING)]:
+        copy.wait_send()
+
+    for d in RING:
+        arrived_col = pltpu.make_async_copy(col_src, col_dst.at[chip(n - d)], col_recv.at[d])
+        arrived_col.wait()
+    for d, x in everyone:
+        arrived(R, d, x, p_dst.at[core(x), chip(n - d)])
     velocity = []
     for b in range(2):
         got = p_dst[b].astype(F32).reshape(n * rows, HEAD).astype(BF16)
         sums, means, squares = [
-            jnp.dot(got, m, preferred_element_type=F32).reshape(n, rows, HEAD) for m in picks
+            jnp.dot(got, m, preferred_element_type=F32).reshape(n, rows, HEAD) for m in (pick_ref[0], pick_ref[1], pick_ref[2])
         ]
         mean = jnp.sum(means, axis=0) / n
         away = means - mean[None]
@@ -276,11 +284,9 @@
         for s in range(n):
             total = total + (sums[s] + away[s] * col_dst[s, 0:1, :])
         velocity.append(total * lax.rsqrt(variance + NORM_EPS))
+    sigma_now, sigma_next = sigmas[0], sigmas[1]
     guide = jnp.where(e == 0, HIGH_GUIDE, LOW_GUIDE)
     guided = (velocity[1] + guide * (velocity[0] - velocity[1]))[:, 0:half]
-    now = jnp.full((rows, half), step[0, 0], jnp.int32).astype(F32)
-    sigma_now = sigma_at(now)
-    sigma_next = sigma_at(now + 1.0)
     step_v[...] = (lat[...] + (sigma_next - sigma_now) * guided).astype(BF16)
     copy = pltpu.make_async_remote_copy(
         step_v, hlat_out.at[0], x_send.at[2], x_recv.at[2], device_id={"expert": 1 - e}, device_id_type=MESH
@@ -290,7 +296,7 @@
     clean_v[...] = lat[...] - sigma_now * guided
     done = pltpu.make_async_copy(clean_v, clean_out.at[0], out_sem)
     done.start()
-    for copy in sends:
+    for copy in sends[4 * len(remote) + len(RING) :]:
         copy.wait_send()
     done.wait()
     for copy in handed:
@@ -353,6 +359,7 @@
             pltpu.VMEM((text, width), BF16), pltpu.VMEM((text, width), BF16),
             pltpu.VMEM((2 * HEAD, width), BF16), pltpu.VMEM((1, HEAD), F32), pltpu.VMEM((n, 1, HEAD), F32),
             pltpu.VMEM((n, 2, rows, HEAD), BF16), pltpu.VMEM((2, n, rows, HEAD), BF16),
+            pltpu.VMEM((3, HEAD, HEAD), BF16), pltpu.VMEM((2, rows, channels), F32),
             pltpu.VMEM((rows, channels), F32), pltpu.VMEM((rows, channels), BF16),
             dma((12,)), dma((5, n, 2)), dma((5, n, 2)), dma((n,)), dma((n,)), dma((3,)), dma((3,)), dma,
         ],

time: 73.5 us -> 73.5 us (level)
  no operation moved by 1% of the time
where the time goes in v4:
time: 73.5 us; the launch traced here: 73.2 us
  Pallas kernels  71.2 us (97%)
  between operations  1.93 us (3%)
    pallas_call x1, Pallas kernels, per_device(): pl.pallas_call(kernel, out_shape=(jax.ShapeDtypeStruct(latent.shape, F32)...  69.4 us
    pallas_call x1, Pallas kernels, per_device(): pl.pallas_call(hand_on, out_shape=tuple((jax.ShapeDtypeStruct(r.shape, r....  1.8 us

profile of v4, /device:TPU:6, one launch (start us, length us, event | category | flops | bytes accessed | tf_op | source)
XLA Modules:
  0.0 73.2 jit_solution(11031955175188947582)
XLA Ops:
  1.9 69.4 %shard_map.156 = (f32[1,40,64]{2,1,0:T(8,128)}, bf16[1,40,64]{2,1,0:T(8,128)(2,1)}, bf16[1,1,256,384]{3,2,1,0:T(8,128)(2,1)}, bf16[1,1,256,384]{3,2,1,0:T(8,128)(2,1)}) custom-call(bf16[1,2,40,3072]{3,2,1,0:T(8,128)(2,1)} %refs_0_.1, bf16[1,2,40,3072]{3,2,1,0:T(8,128)(2,1)} %refs_1_.1, bf16[1,2,40,3072]{3,2,1,0:T(8,128)(2,1)} %refs_2_.1, ...), custom_call_target="tpu_custom_call" | custom-call | flops 1000000000 | bytes 4000000 | tf_op jit(solution)/shard_map/pallas_call | solution.py:339
  71.4 1.8 %shard_map.157 = (f32[1,40,64]{2,1,0:T(8,128)}, bf16[1,40,64]{2,1,0:T(8,128)(2,1)}, bf16[1,1,256,384]{3,2,1,0:T(8,128)(2,1)}, bf16[1,1,256,384]{3,2,1,0:T(8,128)(2,1)}) custom-call(f32[1,40,64]{2,1,0:T(8,128)} %get-tuple-element.8.refs_0_, bf16[1,40,64]{2,1,0:T(8,128)(2,1)} %get-tuple-element.9.refs_1_, bf16[1,1,256,384]{3,2,1,0:T(8,128)(2,1)} %get-tuple-element.10.refs_2_, ...), custom_call_target="tpu_custom_call" | custom-call | tf_op jit(solution)/shard_map/pallas_call | solution.py:373
